TPU v7x, 256 devices: a whole 4x4x8 slice. The times are simulated.
256 devices in a mesh: lon: 64 (over y_lo, z, x), lat: 4 (over y_hi, core).
Axes of the slice: x: 4, y: 4 (y_hi: 2, y_lo: 2; y = y_hi * 2 + y_lo), z: 8, core: 2. Of those that a mesh axis runs over, the one named last changes fastest.
Arguments:
- tokens: bfloat16 [2, 24, 3072, 384], P(None, 'lat', 'lon'), may hold values from -6 to 6
- cotangent: bfloat16 [2, 24, 3072, 384], P(None, 'lat', 'lon'), may hold values from -40 to 40
- mask_ids: int32 [2, 24], P(None, 'lat'), may hold values from 0 to 1
- band_type: int32 [4], replicated, may hold values from 0 to 3, each once
- bias_table: bfloat16 [4, 12, 3312], replicated, may hold values from -4 to 4
- w_qkv: bfloat16 [384, 1152], replicated, may hold values from -0.3125 to 0.3125
- w_proj: bfloat16 [384, 384], replicated, may hold values from -0.3125 to 0.3125
- ln_gain: float32 [384], replicated, may hold values from 0.5 to 1.5
- ln_shift: float32 [384], replicated, may hold values from -1.5 to 1.5
Outputs:
- grad_tokens: bfloat16 [2, 24, 3072, 384], P(None, 'lat', 'lon')
- grad_qkv: bfloat16 [384, 1152], replicated
- grad_proj: bfloat16 [384, 384], replicated
- grad_gain: float32 [384], replicated
- grad_shift: float32 [384], replicated
- grad_table: bfloat16 [4, 12, 3312], replicated
All inputs are finite; a program needn't handle non-finite values.
Results may differ from a plain program's by a relative error of at most 0.0089.
Values may be sent and summed in bfloat16 or wider, within the bound.
A program may use at most 128 MiB of HBM per device.

v0:
```python
import jax
import jax.numpy as jnp
import numpy as np
from jax import lax
from jax.experimental import pallas as pl
from jax.experimental.pallas import tpu as pltpu
from jax.sharding import PartitionSpec as P

WPL, WLAT, WLON = 2, 6, 12
WINDOW = WPL * WLAT * WLON
ROWS = WPL * WLAT
SPREAD = 2 * WLON - 1
EDGE = 16
X_SIZE, Y_SIZE, Z_SIZE = 4, 4, 8
PART = 192
PIECE = 48
SLOT = 16
MESH = pl.DeviceIdType.MESH
GROUP = 4
EPSILON = 1e-05
LOG2E = 1.4426950408889634
BF = jnp.bfloat16
F32 = jnp.float32


def token_route(lon_cols):
    half_lat, half_lon = WLAT // 2, WLON // 2
    windows = lon_cols // WLON
    near = WPL * half_lat * lon_cols
    far = WPL * half_lat * EDGE
    route = np.zeros((windows * WINDOW, 2 * near + 2 * far), np.float32)
    for w in range(windows):
        for o in range(WLON):
            for l in range(WPL):
                for a in range(WLAT):
                    level = (l + 1) % WPL
                    col = w * WLON + o + half_lon
                    row = level * half_lat + a % half_lat
                    if col < lon_cols:
                        source = row * lon_cols + col + (near if a >= half_lat else 0)
                    else:
                        source = 2 * near + row * EDGE + col - lon_cols
                        source += far if a >= half_lat else 0
                    route[w * WINDOW + o * ROWS + l * WLAT + a, source] = 1.0
    return route


def head_order():
    perm = np.zeros((GROUP * WINDOW, GROUP * WINDOW), np.float32)
    for o in range(WLON):
        for h in range(GROUP):
            for r in range(ROWS):
                perm[(o * GROUP + h) * ROWS + r, (h * WLON + o) * ROWS + r] = 1.0
    return perm


def table_order():
    order = np.zeros((SPREAD * ROWS, 512), np.float32)
    for d in range(SPREAD):
        for l in range(WPL):
            for a in range(WLAT):
                order[(SPREAD - 1 - d) * ROWS + l * WLAT + a, l * 256 + a * SPREAD + d] = 1.0
    return order


def row_order(heads):
    order = np.zeros((heads * ROWS, heads * ROWS), np.float32)
    for h in range(heads):
        for r in range(ROWS):
            order[r * heads + h, h * ROWS + r] = 1.0
    return order


def head_blocks(head_dim):
    rows = np.arange(GROUP * head_dim)[:, None] // head_dim
    cols = np.arange(GROUP * WINDOW)[None, :] // WINDOW
    return (rows == cols).astype(np.float32)


def gather_heads():
    return np.tile(np.eye(WINDOW, dtype=np.float32), (1, GROUP))


def nn(a, b):
    return lax.dot_general(a, b, (((1,), (0,)), ((), ())), preferred_element_type=F32)


def nt(a, b):
    return lax.dot_general(a, b, (((1,), (1,)), ((), ())), preferred_element_type=F32)


def tn(a, b):
    return lax.dot_general(a, b, (((0,), (0,)), ((), ())), preferred_element_type=F32)


def place():
    lon = lax.axis_index("lon")
    lat = lax.axis_index("lat")
    x = lax.rem(lon, X_SIZE)
    z = lax.rem(lon // X_SIZE, Z_SIZE)
    y = (lat // 2) * 2 + lon // (X_SIZE * Z_SIZE)
    return x, y, z, lax.rem(lat, 2)


def device(x, y, z, core):
    return ((lax.rem(y, 2) * Z_SIZE + z) * X_SIZE + x, (y // 2) * 2 + core)


def whole_kernel(
    ids, types, tokens, cotangent, table_h, w_qkv_h, w_proj_h, gain_v, shift_v,
    route_h, unroute_h, perm_h, order_h, blocks_h, gather_h, reorder_h,
    o_tokens, o_full, o_small,
    cat, edge, cot_own, joined, table, w_qkv, w_proj, route, unroute, perm, order, blocks, gather, reorder,
    tall, folded, bias, d_bias, normed, inv, ln, ln_t, cot, qkv, d_att, att, d_qkv,
    d_main, d_edge, back_main, back_edge,
    grads, tables, core_in, s1_out, s1_in, s2_out, s2_in, z_in, full, small, small_core, small_x, small_y, small_z,
    load_s, out_s, halo_s, halo_r, back_s, back_r, core_s, core_r, s1_s, s1_r, s2_s, s2_r, z_s, z_r, g2_s, g2_r, g1_s, g1_r,
    sib_s, sib_r, mc_s, mc_r, mx_s, mx_r, my_s, my_r, mz_s, mz_r,
):
    half_lat = WLAT // 2
    half_lon = WLON // 2
    lon_cols = tokens.shape[2]
    channels = tokens.shape[3]
    main = 2 * WPL * half_lat * lon_cols
    groups = channels // 128
    heads = groups * GROUP
    windows = lon_cols // WLON
    span = GROUP * WINDOW
    head_dim = 128 // GROUP
    scale = head_dim ** -0.5
    x, y, z, core = place()
    other = 1 - core
    beside = x + 1 - 2 * lax.rem(x, 2)
    across = lax.rem(y + 2, Y_SIZE)
    y_up = lax.rem(y + 2 * other, Y_SIZE)
    y_down = lax.rem(y + 2 * core, Y_SIZE)
    sibling = device(x, y, z, other)

    loads = [
        pltpu.make_async_copy(src, dst, load_s.at[i])
        for i, (src, dst) in enumerate((
            (table_h, table), (order_h, order), (reorder_h, reorder), (perm_h, perm),
            (tokens.at[:, pl.ds(half_lat, half_lat)], cat.at[0, :, :, :, pl.ds(0, channels)]),
            (cotangent.at[:, pl.ds(half_lat, half_lat)], cat.at[0, :, :, :, pl.ds(channels, channels)]),
            (route_h, route), (w_proj_h, w_proj), (blocks_h, blocks), (gather_h, gather),
            (unroute_h, unroute), (cotangent, cot_own),
            *(
                (
                    w_qkv_h.at[:, pl.ds(b * channels + g * 128, 128)],
                    w_qkv.at[:, pl.ds((3 * g + b) * 128, 128)],
                )
                for g in range(groups)
                for b in range(3)
            ),
        ))
    ]
    for load in loads:
        load.start()

    barrier = pltpu.get_barrier_semaphore()
    friends = [sibling, device(x, across, z, other), device(beside, y, z, other), device(beside, across, z, other)]
    friends += [device(lax.rem(x + i, X_SIZE), y, z, core) for i in range(1, X_SIZE)]
    friends += [device(x, lax.rem(y + i, Y_SIZE), z, core) for i in range(1, Y_SIZE)]
    friends += [device(x, y, lax.rem(z + i, Z_SIZE), core) for i in range(1, Z_SIZE)]
    for friend in friends:
        pl.semaphore_signal(barrier, inc=1, device_id=friend, device_id_type=MESH)
    pl.semaphore_wait(barrier, len(friends))

    def remote(src, dst, send, recv, target):
        return pltpu.make_async_remote_copy(
            src_ref=src, dst_ref=dst, send_sem=send, recv_sem=recv, device_id=target, device_id_type=MESH
        )

    first, last = pl.ds(0, half_lat), pl.ds(half_lat, half_lat)
    halos = []
    for i, array in enumerate((tokens, cotangent)):
        lanes = pl.ds(i * channels, channels)
        up = device(x, y_up, z, other)
        halos += [
            (array.at[:, first], cat.at[1, :, :, :, lanes], up),
            (array.at[:, last, pl.ds(0, EDGE)], edge.at[0, :, :, :, lanes], device(beside, y, z, core)),
            (array.at[:, first, pl.ds(0, EDGE)], edge.at[1, :, :, :, lanes], device(beside, y_up, z, other)),
        ]
    halos = [remote(src, dst, halo_s.at[i], halo_r.at[i], to) for i, (src, dst, to) in enumerate(halos)]
    for copy in halos:
        copy.start()

    for load in loads[:4]:
        load.wait()
    own_type = types[lax.axis_index("lat")]
    picked = (lax.broadcasted_iota(jnp.int32, (1, 4, 1), 1) == own_type).astype(F32)
    rows_of_type = jnp.sum(table[...].astype(F32) * picked, axis=1)
    tall[...] = jnp.zeros_like(tall)
    for lq in range(WPL):
        for lk in range(WPL):
            for a in range(WLAT):
                start = ((lq * WPL + lk) * WLAT + a) * WLAT * SPREAD
                row = (lq * WLAT + a) * heads
                tall[row : row + heads, lk * 256 : lk * 256 + WLAT * SPREAD] = rows_of_type[:, start : start + WLAT * SPREAD]
    laid = nt(order[...], tall[...].astype(BF)).astype(BF)
    folded[...] = nn(laid, reorder[...])
    lane = lax.rem(lax.broadcasted_iota(jnp.int32, (1, span), 1), ROWS)
    sub = lax.rem(lax.broadcasted_iota(jnp.int32, (WINDOW, 1), 0), ROWS)
    id_q = jnp.zeros((1, span), jnp.int32)
    id_k = jnp.zeros((WINDOW, 1), jnp.int32)
    for l in range(WPL):
        for a in range(WLAT):
            value = ids[l, a]
            id_q = jnp.where(lane == l * WLAT + a, value, id_q)
            id_k = jnp.where(sub == l * WLAT + a, value, id_k)
    masked = jnp.where(id_k == id_q, 0.0, -1e30)
    for g in range(groups):
        pieces = [
            folded[(WLON - 1 - o) * ROWS : (WLON - 1 - o) * ROWS + WINDOW, g * GROUP * ROWS : (g + 1) * GROUP * ROWS]
            for o in range(WLON)
        ]
        spread = jnp.concatenate(pieces, axis=1).astype(BF)
        bias[g] = nn(spread, perm[...]) * LOG2E + masked

    gain = gain_v[...].reshape(1, channels)
    shift = shift_v[...].reshape(1, channels)
    for load in loads[4:]:
        load.wait()
    for copy in halos[:3]:
        copy.wait_recv()
    x_in = nn(route[:, :main], cat[..., :channels].reshape(main, channels))
    x_in = x_in + nn(route[:, main:], edge[..., :channels].reshape(-1, channels))
    average = jnp.mean(x_in, axis=1, keepdims=True)
    centred = x_in - average
    variance = jnp.mean(centred * centred, axis=1, keepdims=True)
    inv_std = lax.rsqrt(variance + EPSILON)
    inv[...] = inv_std
    norm = centred * inv_std
    normed[...] = norm
    ln_out = (norm * gain + shift).astype(BF)
    ln[...] = ln_out
    ln_t[...] = ln_out.T
    qkv[...] = nn(ln[...], w_qkv[...]).astype(BF)
    for copy in halos[3:]:
        copy.wait_recv()
    moved = nn(route[:, :main], cat[..., channels:].reshape(main, channels))
    moved = moved + nn(route[:, main:], edge[..., channels:].reshape(-1, channels))
    cot[...] = moved.astype(BF)
    d_att[...] = nt(cot[...], w_proj[...]).astype(BF)

    lanes = lax.broadcasted_iota(jnp.int32, (1, 128), 1) // head_dim
    own = [(lanes == h).astype(F32).astype(BF) for h in range(GROUP)]
    eye = (
        lax.broadcasted_iota(jnp.int32, (128, 128), 0) == lax.broadcasted_iota(jnp.int32, (128, 128), 1)
    ).astype(F32).astype(BF)

    def attend(g, w):
        rows = pl.ds(pl.multiple_of(w * WINDOW, WINDOW), WINDOW)
        q_cols, k_cols, v_cols = (slice((3 * g + b) * 128, (3 * g + b + 1) * 128) for b in range(3))
        cols = slice(g * 128, (g + 1) * 128)
        q, k, v, da = qkv[rows, q_cols], qkv[rows, k_cols], qkv[rows, v_cols], d_att[rows, cols]
        q_heads = jnp.concatenate([q * own[h] for h in range(GROUP)], axis=0)
        da_heads = jnp.concatenate([da * own[h] for h in range(GROUP)], axis=0)
        raised = jnp.exp2(nt(k, q_heads) * (scale * LOG2E) + bias[g])
        probs = raised * (1.0 / jnp.sum(raised, axis=0, keepdims=True))
        probs_b = probs.astype(BF)
        v_t = nt(eye, v).astype(BF)
        k_t = nt(eye, k).astype(BF)
        weighted = probs * nt(v, da_heads)
        d_scores = weighted - probs * jnp.sum(weighted, axis=0, keepdims=True)
        d_scores_b = d_scores.astype(BF)
        mask = blocks[...]
        att_t = nn(v_t, probs_b).astype(BF) * mask
        dq_t = (nn(k_t, d_scores_b) * scale).astype(BF) * mask

        def store():
            att[rows, cols] = nt(gather[...], att_t).astype(BF)
            d_qkv[rows, q_cols] = nt(gather[...], dq_t).astype(BF)
            d_qkv[rows, k_cols] = (nn(d_scores_b, q_heads) * scale).astype(BF)
            d_qkv[rows, v_cols] = nn(probs_b, da_heads).astype(BF)

        return d_scores, store

    def two_windows(g, w):
        left, store_left = attend(g, w)
        right, store_right = attend(g, w + 1)
        store_left()
        store_right()
        return left + right

    def gradients(g):
        weights = nn(ln_t[...], d_qkv[:, 3 * g * 128 : 3 * (g + 1) * 128]).astype(BF)
        for b in range(3):
            grads[g, b] = weights[:, b * 128 : (b + 1) * 128]
        proj = tn(att[:, g * 128 : (g + 1) * 128], cot[...]).astype(BF)
        for t in range(groups):
            grads[g, 3, t * 128 : (t + 1) * 128] = proj[:, t * 128 : (t + 1) * 128]
        high = d_bias[...].astype(BF)
        low = (d_bias[...] - high.astype(F32)).astype(BF)
        spread = nt(high, perm[...]) + nt(low, perm[...])
        folded[:, :128] = jnp.zeros((folded.shape[0], 128), F32)
        for o in range(WLON):
            start = (WLON - 1 - o) * ROWS
            folded[start : start + WINDOW, : GROUP * ROWS] += spread[:, o * GROUP * ROWS : (o + 1) * GROUP * ROWS]
        rows = tn(folded[:, : GROUP * ROWS].astype(BF), order[...]).astype(BF)
        tables[g] = jnp.zeros(tables.shape[1:], BF)
        for t in range(4):
            part = rows[:, t * 128 : (t + 1) * 128]
            for i in range(3):
                slot = 3 * t + i
                tables[g, slot // 4, slot % 4] = part[i * SLOT : (i + 1) * SLOT]

    p1 = jnp.where(core == 0, x, y)
    p2 = jnp.where(core == 0, y, x)

    def on1(p):
        return device(jnp.where(core == 0, p, x), jnp.where(core == 0, y, p), z, core)

    def on2(p):
        return device(jnp.where(core == 0, x, p), jnp.where(core == 0, p, y), z, core)

    def after1(i):
        return lax.rem(p1 + i, 4)

    def after2(i):
        return lax.rem(p2 + i, 4)

    def core_copy(g):
        return remote(grads.at[g, pl.ds(2 * other, 2)], core_in.at[g], core_s.at[g], core_r.at[g], sibling)

    def s1_copy(g, peer):
        return remote(s1_out.at[g, peer], s1_in.at[g, p1], s1_s.at[g, peer], s1_r.at[g, p1], on1(peer))

    def s1_take(g, peer):
        return remote(s1_out.at[g, peer], s1_in.at[g, peer], s1_s.at[g, peer], s1_r.at[g, peer], on1(peer))

    def s2_copy(g, peer):
        return remote(s2_out.at[g, peer], s2_in.at[g, p2], s2_s.at[g, peer], s2_r.at[g, p2], on2(peer))

    def s2_take(g, peer):
        return remote(s2_out.at[g, peer], s2_in.at[g, peer], s2_s.at[g, peer], s2_r.at[g, peer], on2(peer))

    def z_copy(g, peer, slot):
        return remote(z_in.at[g, slot], z_in.at[g, slot], z_s.at[g, peer], z_r.at[g, slot], device(x, y, peer, core))

    def g2_copy(g, peer, slot):
        here = full.at[g, core, p1, slot]
        return remote(here, here, g2_s.at[g, peer], g2_r.at[g, slot], on2(peer))

    def g1_copy(g, peer, slot):
        here = full.at[g, core, slot]
        return remote(here, here, g1_s.at[g, peer], g1_r.at[g, slot], on1(peer))

    def sib_copy(g, half, slot):
        here = full.at[g, half, slot]
        return remote(here, here, sib_s.at[g, slot], sib_r.at[g, slot], sibling)

    def step0(g):
        core_copy(g).start()

    def step1(g):
        core_copy(g).wait_recv()
        for j in range(4):
            rows = slice((j % 2) * PART, (j % 2 + 1) * PART)
            added = grads[g, 2 * core + j // 2, rows].astype(F32) + core_in[g, j // 2, rows].astype(F32)
            s1_out[g, j, :PART] = added.astype(BF)
            s1_out[g, j, PART:] = tables[g, j].reshape(4 * SLOT, 128)
        for i in (2, 1, 3):
            s1_copy(g, after1(i)).start()

    def step2(g):
        def split(part, source):
            high = jnp.where(core == 0, y, source) // 2
            low_rows = jnp.where(high == 0, part[PART:], jnp.zeros_like(part[PART:]))
            return part[:PART], low_rows, part[PART:] - low_rows

        w, t0, t1 = split(s1_out[g, p1].astype(F32), p1)
        for i in (1, 3, 2):
            source = after1(i)
            s1_take(g, source).wait_recv()
            more = split(s1_in[g, source].astype(F32), source)
            w, t0, t1 = w + more[0], t0 + more[1], t1 + more[2]
        for j in range(4):
            s2_out[g, j] = jnp.concatenate(
                [w[j * PIECE : (j + 1) * PIECE], t0[j * SLOT : (j + 1) * SLOT], t1[j * SLOT : (j + 1) * SLOT]], axis=0
            ).astype(BF)
        for i in (2, 1, 3):
            s2_copy(g, after2(i)).start()

    def step3(g):
        total = s2_out[g, p2].astype(F32)
        for i in (1, 3, 2):
            source = after2(i)
            s2_take(g, source).wait_recv()
            total = total + s2_in[g, source].astype(F32)
        z_in[g, z] = total.astype(BF)
        for i in (4, 3, 5, 2, 6, 1, 7):
            z_copy(g, lax.rem(z + i, Z_SIZE), z).start()

    def step4(g):
        for i in (1, 7, 2, 6, 3, 5, 4):
            source = lax.rem(z + i, Z_SIZE)
            z_copy(g, source, source).wait_recv()
        total = z_in[g, 0].astype(F32)
        for i in range(1, Z_SIZE):
            total = total + z_in[g, i].astype(F32)
        full[g, core, p1, p2] = total.astype(BF)
        for i in (2, 1, 3):
            g2_copy(g, after2(i), p2).start()

    def step5(g):
        for i in (1, 3, 2):
            source = after2(i)
            g2_copy(g, source, source).wait_recv()
        for i in (2, 1, 3):
            g1_copy(g, after1(i), p1).start()
        sib_copy(g, core, p1).start()

    def step6(g):
        for i in (1, 3, 2):
            source = after1(i)
            g1_copy(g, source, source).wait_recv()
            sib_copy(g, core, source).start()

    def step7(g):
        for i in range(4):
            sib_copy(g, other, i).wait_recv()
        full_copy(g).start()

    def full_copy(g):
        return pltpu.make_async_copy(full.at[g], o_full.at[g], out_s.at[g])

    def tokens_copy():
        return pltpu.make_async_copy(joined, o_tokens, out_s.at[groups])

    def finish(g):
        core_copy(g).wait_send()
        for i in range(1, 4):
            s1_copy(g, after1(i)).wait_send()
            s2_copy(g, after2(i)).wait_send()
            g2_copy(g, after2(i), p2).wait_send()
            g1_copy(g, after1(i), p1).wait_send()
        for i in range(1, Z_SIZE):
            z_copy(g, lax.rem(z + i, Z_SIZE), z).wait_send()
        for i in range(4):
            sib_copy(g, core, i).wait_send()

    def mc_copy():
        return remote(small, small_core, mc_s.at[0], mc_r.at[0], sibling)

    def mx_copy(peer, slot):
        return remote(small_x.at[slot], small_x.at[slot], mx_s.at[peer], mx_r.at[slot], device(peer, y, z, core))

    def my_copy(peer, slot):
        return remote(small_y.at[slot], small_y.at[slot], my_s.at[peer], my_r.at[slot], device(x, peer, z, core))

    def mz_copy(peer, slot):
        return remote(small_z.at[slot], small_z.at[slot], mz_s.at[peer], mz_r.at[slot], device(x, y, peer, core))

    def small_share(copy, buffer, place_here, size, value):
        buffer[place_here] = value
        for i in range(1, size):
            copy(lax.rem(place_here + i, size), place_here).start()

    def small_sum(copy, buffer, place_here, size):
        for i in range(1, size):
            source = lax.rem(place_here + i, size)
            copy(source, source).wait_recv()
        total = buffer[0]
        for i in range(1, size):
            total = total + buffer[i]
        return total

    def small_finish():
        mc_copy().wait_send()
        for copy, here, size in ((mx_copy, x, X_SIZE), (my_copy, y, Y_SIZE), (mz_copy, z, Z_SIZE)):
            for i in range(1, size):
                copy(lax.rem(here + i, size), here).wait_send()

    def group(g, between):
        d_bias[...] = two_windows(g, 0)
        between()
        d_bias[...] += two_windows(g, 2)
        gradients(g)
        step0(g)

    def mid1():
        step1(0)

    def mid2():
        step1(1)
        step2(0)

    group(0, lambda: None)
    group(1, mid1)
    group(2, mid2)
    step3(0)
    step2(1)
    step1(2)

    d_ln = nt(d_qkv[...], w_qkv[...])
    norm = normed[...]
    small[...] = jnp.zeros_like(small)
    for g in range(groups):
        cols = slice(g * 128, (g + 1) * 128)
        small[g : g + 1] = jnp.sum(d_ln[:, cols] * norm[:, cols], axis=0, keepdims=True)
        small[groups + g : groups + g + 1] = jnp.sum(d_ln[:, cols], axis=0, keepdims=True)
    mc_copy().start()
    scaled = d_ln * gain
    d_flat = inv[...] * (
        scaled
        - jnp.mean(scaled, axis=1, keepdims=True)
        - norm * jnp.mean(scaled * norm, axis=1, keepdims=True)
    )
    d_flat = d_flat.astype(BF)
    d_main[...] = nn(unroute[:main], d_flat).astype(BF).reshape(d_main.shape)
    d_edge[...] = nn(unroute[main:], d_flat).astype(BF).reshape(d_edge.shape)
    backs = [
        remote(d_main.at[1], back_main, back_s.at[0], back_r.at[0], device(x, y_down, z, other)),
        remote(d_edge.at[0], back_edge.at[0], back_s.at[1], back_r.at[1], device(beside, y, z, core)),
        remote(d_edge.at[1], back_edge.at[1], back_s.at[2], back_r.at[2], device(beside, y_down, z, other)),
    ]
    for copy in backs:
        copy.start()
    step3(1)
    step2(2)
    mc_copy().wait_recv()
    small_share(mx_copy, small_x, x, X_SIZE, small[...] + small_core[...])
    step4(0)
    step3(2)
    small_share(my_copy, small_y, y, Y_SIZE, small_sum(mx_copy, small_x, x, X_SIZE))
    step5(0)
    small_share(mz_copy, small_z, z, Z_SIZE, small_sum(my_copy, small_y, y, Y_SIZE))

    for copy in backs:
        copy.wait_recv()
    for l in range(WPL):
        for a in range(WLAT):
            if a < half_lat:
                inner, outer = back_main[l, a], back_edge[1, l, a]
            else:
                inner, outer = d_main[0, l, a - half_lat], back_edge[0, l, a - half_lat]
            value = cot_own[l, a].astype(F32) + inner.astype(F32)
            joined[l, a, EDGE:] = value[EDGE:].astype(BF)
            joined[l, a, :EDGE] = (value[:EDGE] + outer.astype(F32)).astype(BF)
    tokens_copy().start()
    step4(1)
    step6(0)
    step4(2)
    step5(1)
    step7(0)
    o_small[...] = small_sum(mz_copy, small_z, z, Z_SIZE)
    step5(2)
    step6(1)
    step7(1)
    step6(2)
    step7(2)

    for copy in halos + backs:
        copy.wait_send()
    for g in range(groups):
        finish(g)
    small_finish()
    tokens_copy().wait()
    for g in range(groups):
        full_copy(g).wait()


def assemble_kernel(
    types, full_h, joined_h, small, reorder,
    o_tokens, o_qkv, o_proj, o_table, o_gain, o_shift,
    full, wide, typed, sem,
):
    channels = o_proj.shape[0]
    groups = channels // 128
    heads = groups * GROUP
    loads = [pltpu.make_async_copy(full_h.at[g], full.at[g], sem.at[g]) for g in range(groups)]
    through = pltpu.make_async_copy(joined_h, o_tokens, sem.at[groups])
    for load in loads:
        load.start()
    through.start()
    o_gain[...] = jnp.concatenate([small[g : g + 1] for g in range(groups)], axis=1).reshape(channels)
    o_shift[...] = jnp.concatenate([small[g : g + 1] for g in range(groups, 2 * groups)], axis=1).reshape(channels)
    for g in range(groups):
        loads[g].wait()
        for half in range(2):
            for j in range(4):
                for i in range(4):
                    part = full[g, half, j, i, :PIECE]
                    block = 2 * half + j // 2
                    row = (j % 2) * PART + i * PIECE
                    if block < 3:
                        cols = slice(block * channels + g * 128, block * channels + (g + 1) * 128)
                        o_qkv[row : row + PIECE, cols] = part
                    else:
                        for u in range(0, PIECE, SLOT):
                            at = row + u
                            tile = at // 128
                            o_proj[g * 128 + at % 128 : g * 128 + at % 128 + SLOT, tile * 128 : (tile + 1) * 128] = (
                                part[u : u + SLOT]
                            )

    for b in range(4):
        at = PIECE + (b // 2) * SLOT
        for t in range(4):
            stacked = jnp.concatenate(
                [
                    full[g, b % 2, slot // 4, slot % 4, at : at + SLOT]
                    for g in range(groups)
                    for slot in range(3 * t, 3 * t + 3)
                ],
                axis=0,
            )
            wide[b, :, t * 128 : (t + 1) * 128] = nn(reorder[...], stacked)
    for kind in range(4):
        band = jnp.int32(0)
        for b in range(1, 4):
            band = jnp.where(types[b] == kind, b, band)
        table_rows = wide[band]
        parts = []
        for lq in range(WPL):
            for lk in range(WPL):
                for a in range(WLAT):
                    row = (lq * WLAT + a) * heads
                    parts.append(table_rows[row : row + heads, lk * 256 : lk * 256 + WLAT * SPREAD])
        typed[:, kind, :] = jnp.concatenate(parts, axis=1)
    o_table[...] = typed[...].astype(BF)
    through.wait()


def local(tokens, cotangent, mask_ids, band_type, bias_table, w_qkv, w_proj, ln_gain, ln_shift):
    lon_cols, channels = tokens.shape[2:]
    groups = channels // 128
    heads = groups * GROUP
    half_lat = WLAT // 2
    count = WPL * WLAT * lon_cols
    span = GROUP * WINDOW
    route = token_route(lon_cols)
    constants = [
        jnp.asarray(c, BF)
        for c in (
            route, route.T, head_order(), table_order(), head_blocks(128 // GROUP), gather_heads(), row_order(heads)
        )
    ]
    anywhere = pl.BlockSpec(memory_space=pl.ANY)
    scalars = pl.BlockSpec(memory_space=pltpu.SMEM)
    vmem = pl.BlockSpec(memory_space=pltpu.VMEM)
    dma = pltpu.SemaphoreType.DMA
    bf = lambda *shape: pltpu.VMEM(shape, BF)
    f32 = lambda *shape: pltpu.VMEM(shape, F32)
    pairs = lambda *shape: [dma(shape), dma(shape)]
    pieces = (groups, 2, 4, 4, PIECE + 2 * SLOT, 128)
    table = bias_table.transpose(1, 0, 2)
    joined, full, small = pl.pallas_call(
        whole_kernel,
        out_shape=(
            jax.ShapeDtypeStruct(tokens.shape, BF),
            jax.ShapeDtypeStruct(pieces, BF),
            jax.ShapeDtypeStruct((8, 128), F32),
        ),
        in_specs=[scalars] * 2 + [anywhere] * 5 + [vmem] * 2 + [anywhere] * 7,
        out_specs=(anywhere, anywhere, vmem),
        scratch_shapes=[
            bf(2, WPL, half_lat, lon_cols, 2 * channels),
            bf(2, WPL, half_lat, EDGE, 2 * channels),
            bf(*tokens.shape),
            bf(*tokens.shape),
            bf(*table.shape),
            bf(channels, 3 * channels),
            bf(channels, channels),
            *[bf(*c.shape) for c in constants],
            f32(heads * ROWS, 512),
            f32(SPREAD * ROWS, heads * ROWS),
            f32(groups, WINDOW, span),
            f32(WINDOW, span),
            f32(count, channels),
            f32(count, 1),
            bf(count, channels),
            bf(channels, count),
            bf(count, channels),
            bf(count, 3 * channels),
            bf(count, channels),
            bf(count, channels),
            bf(count, 3 * channels),
            bf(2, WPL, half_lat, lon_cols, channels),
            bf(2, WPL, half_lat, EDGE, channels),
            bf(WPL, half_lat, lon_cols, channels),
            bf(2, WPL, half_lat, EDGE, channels),
            bf(groups, 4, channels, 128),
            bf(groups, 4, 4, SLOT, 128),
            bf(groups, 2, channels, 128),
            bf(groups, 4, PART + 4 * SLOT, 128),
            bf(groups, 4, PART + 4 * SLOT, 128),
            bf(groups, 4, PIECE + 2 * SLOT, 128),
            bf(groups, 4, PIECE + 2 * SLOT, 128),
            bf(groups, Z_SIZE, PIECE + 2 * SLOT, 128),
            bf(*pieces),
            f32(8, 128),
            f32(8, 128),
            f32(X_SIZE, 8, 128),
            f32(Y_SIZE, 8, 128),
            f32(Z_SIZE, 8, 128),
            dma((12 + 3 * groups,)),
            dma((groups + 1,)),
            *pairs(6), *pairs(3), *pairs(groups), *pairs(groups, 4), *pairs(groups, 4), *pairs(groups, Z_SIZE),
            *pairs(groups, 4), *pairs(groups, 4), *pairs(groups, 4),
            *pairs(1), *pairs(X_SIZE), *pairs(Y_SIZE), *pairs(Z_SIZE),
        ],
        compiler_params=pltpu.CompilerParams(
            collective_id=0, has_side_effects=True, vmem_limit_bytes=56 * 1024 * 1024
        ),
        cost_estimate=pl.CostEstimate(flops=6_000_000_000, bytes_accessed=10_000_000, transcendentals=1_000_000),
    )(mask_ids, band_type, tokens, cotangent, table, w_qkv, w_proj, ln_gain, ln_shift, *constants)
    d_tokens, g_qkv, g_proj, g_table, g_gain, g_shift = pl.pallas_call(
        assemble_kernel,
        out_shape=(
            jax.ShapeDtypeStruct(tokens.shape, BF),
            jax.ShapeDtypeStruct((channels, 3 * channels), BF),
            jax.ShapeDtypeStruct((channels, channels), BF),
            jax.ShapeDtypeStruct(table.shape, BF),
            jax.ShapeDtypeStruct((channels,), F32),
            jax.ShapeDtypeStruct((channels,), F32),
        ),
        in_specs=[scalars, anywhere, anywhere, vmem, vmem],
        out_specs=(anywhere, vmem, vmem, vmem, vmem, vmem),
        scratch_shapes=[
            bf(*pieces),
            f32(4, heads * ROWS, 512),
            f32(*table.shape),
            dma((groups + 1,)),
        ],
        compiler_params=pltpu.CompilerParams(vmem_limit_bytes=40 * 1024 * 1024),
        cost_estimate=pl.CostEstimate(flops=100_000_000, bytes_accessed=6_000_000, transcendentals=0),
    )(band_type, full, joined, small, constants[-1])
    return d_tokens, g_qkv, g_proj, g_gain, g_shift, g_table.transpose(1, 0, 2)


def solution(mesh):
    placed = (P(None, "lat", "lon", None),) * 2 + (P(None, "lat"),) + (P(),) * 6
    return jax.shard_map(
        local,
        mesh=mesh,
        in_specs=placed,
        out_specs=(P(None, "lat", "lon", None), P(), P(), P(), P(), P()),
        check_vma=False,
    )
```

profile of v0, /device:TPU:1, one launch (start us, length us, event | category | flops | bytes accessed | tf_op | source)
XLA Modules:
  0.0 72.7 jit_solution(16411393906267313530)
XLA Ops:
  0.6 0.0 copy-start.2
  0.6 0.0 copy-start.4
  0.7 65.1 %shard_map.199 = (bf16[2,6,48,384]{3,2,1,0:T(8,128)(2,1)}, bf16[3,2,4,4,80,128]{5,4,3,2,1,0:T(8,128)(2,1)}, f32[8,128]{1,0:T(8,128)}) custom-call(s32[2,6]{1,0:T(2,128)} %ids.1, s32[4]{0:T(128)} %types.3, bf16[2,6,48,384]{3,2,1,0:T(8,128)(2,1)} %tokens.1, bf16[2,6,48,384]{3,2,1,0:T(8,128)(2,1)} %cotangent.1, bf16[12,4,3312]{2,1,0:T(4,128)(2,1)} %bitcast.2, ...), custom_call_target="tpu_custom_call" | custom-call | flops 6000000000 | bytes 10000000 | tf_op jit(solution)/shard_map/pallas_call | solution.py:649
  65.8 0.0 copy-done.2
  65.8 0.0 copy-done.4
  65.8 0.0 copy-start
  65.8 1.5 %copy-done = bf16[3,2,4,4,80,128]{5,4,3,2,1,0:T(8,128)(2,1)S(1)} copy-done((bf16[3,2,4,4,80,128]{5,4,3,2,1,0:T(8,128)(2,1)S(1)}, bf16[3,2,4,4,80,128]{5,4,3,2,1,0:T(8,128)(2,1)}, u32[]{:S(2)}) %copy-start) | copy-done | bytes 1966104
  67.4 0.0 copy-start.1
  67.4 1.0 %copy-done.1 = bf16[2,6,48,384]{3,2,1,0:T(8,128)(2,1)S(1)} copy-done((bf16[2,6,48,384]{3,2,1,0:T(8,128)(2,1)S(1)}, bf16[2,6,48,384]{3,2,1,0:T(8,128)(2,1)}, u32[]{:S(2)}) %copy-start.1) | copy-done | bytes 442392
  68.4 0.0 copy-start.3
  68.4 0.7 copy-done.3
  69.0 3.5 %shard_map.200 = (bf16[2,6,48,384]{3,2,1,0:T(8,128)(2,1)}, bf16[384,1152]{1,0:T(8,128)(2,1)}, bf16[384,384]{1,0:T(8,128)(2,1)}, bf16[12,4,3312]{2,1,0:T(4,128)(2,1)}, f32[384]{0:T(512)}, /*index=5*/f32[384]{0:T(512)}) custom-call(s32[4]{0:T(128)S(1)} %copy-done.4, bf16[3,2,4,4,80,128]{5,4,3,2,1,0:T(8,128)(2,1)S(1)} %copy-done, ...), custom_call_target="tpu_custom_call" | custom-call | flops 100000000 | bytes 6000000 | tf_op jit(solution)/shard_map/pallas_call | solution.py:709
Async XLA Ops:
  0.6 65.2 %copy-start.2 = (bf16[144,144]{1,0:T(8,128)(2,1)S(1)}, bf16[144,144]{1,0:T(8,128)(2,1)}, u32[]{:S(2)}) copy-start(bf16[144,144]{1,0:T(8,128)(2,1)} %constant.20.clone.reorder_h.reorder) | copy-start | bytes 124420
  0.6 65.2 %copy-start.4 = (s32[4]{0:T(128)S(1)}, s32[4]{0:T(128)}, u32[]{:S(2)}) copy-start(s32[4]{0:T(128)} %types.3) | copy-start | bytes 52
  65.8 1.5 %copy-start = (bf16[3,2,4,4,80,128]{5,4,3,2,1,0:T(8,128)(2,1)S(1)}, bf16[3,2,4,4,80,128]{5,4,3,2,1,0:T(8,128)(2,1)}, u32[]{:S(2)}) copy-start(bf16[3,2,4,4,80,128]{5,4,3,2,1,0:T(8,128)(2,1)} %get-tuple-element.15.full_h) | copy-start | bytes 5898244
  67.4 1.0 %copy-start.1 = (bf16[2,6,48,384]{3,2,1,0:T(8,128)(2,1)S(1)}, bf16[2,6,48,384]{3,2,1,0:T(8,128)(2,1)}, u32[]{:S(2)}) copy-start(bf16[2,6,48,384]{3,2,1,0:T(8,128)(2,1)} %get-tuple-element.16.joined_h) | copy-start | bytes 1327108
  68.4 0.7 copy-start.3
where the time goes:
time: 72.9 us; the launch traced here: 72.7 us
  Pallas kernels  68.6 us (94%)
  local copies, waits for them, and re-layouts  3.23 us (4%)
  between operations  0.85 us (1%)
    pallas_call x1, Pallas kernels, local(): pl.pallas_call(whole_kernel, out_shape=(jax.ShapeDtypeStruct(tokens.shape...  65.1 us
    pallas_call x1, Pallas kernels, local(): pl.pallas_call(assemble_kernel, out_shape=(jax.ShapeDtypeStruct(tokens.sh...  3.49 us
    unnamed x10, local copies, waits for them, and re-layouts  3.23 us

commit v1 on v0

--- a/solution.py
+++ b/solution.py
@@ -15,6 +15,7 @@
 PART = 192
 PIECE = 48
 SLOT = 16
+UNIT = 8
 MESH = pl.DeviceIdType.MESH
 GROUP = 4
 EPSILON = 1e-05
@@ -154,9 +155,6 @@
             ),
         ))
     ]
-    for load in loads:
-        load.start()
-
     barrier = pltpu.get_barrier_semaphore()
     friends = [sibling, device(x, across, z, other), device(beside, y, z, other), device(beside, across, z, other)]
     friends += [device(lax.rem(x + i, X_SIZE), y, z, core) for i in range(1, X_SIZE)]
@@ -164,6 +162,8 @@
     friends += [device(x, y, lax.rem(z + i, Z_SIZE), core) for i in range(1, Z_SIZE)]
     for friend in friends:
         pl.semaphore_signal(barrier, inc=1, device_id=friend, device_id_type=MESH)
+    for load in loads:
+        load.start()
     pl.semaphore_wait(barrier, len(friends))
 
     def remote(src, dst, send, recv, target):
@@ -297,13 +297,17 @@
         for o in range(WLON):
             start = (WLON - 1 - o) * ROWS
             folded[start : start + WINDOW, : GROUP * ROWS] += spread[:, o * GROUP * ROWS : (o + 1) * GROUP * ROWS]
-        rows = tn(folded[:, : GROUP * ROWS].astype(BF), order[...]).astype(BF)
-        tables[g] = jnp.zeros(tables.shape[1:], BF)
-        for t in range(4):
-            part = rows[:, t * 128 : (t + 1) * 128]
-            for i in range(3):
-                slot = 3 * t + i
-                tables[g, slot // 4, slot % 4] = part[i * SLOT : (i + 1) * SLOT]
+        rows = tn(folded[:, : GROUP * ROWS].astype(BF), order[...])
+        rest = WLAT * SPREAD - 128
+        ends = jnp.concatenate([rows[:, 128 : 128 + rest], rows[:, 384 : 384 + rest]], axis=1)
+        count = GROUP * ROWS // UNIT
+        packed = [ends[i * UNIT : (i + 1) * UNIT] for i in range(count)]
+        packed = jnp.concatenate([*packed, jnp.zeros((UNIT, 128 - count * 2 * rest), F32)], axis=1)
+        laid = jnp.concatenate(
+            [rows[:, :128], rows[:, 256:384], packed, jnp.zeros((16 * UNIT - (2 * count + 1) * UNIT, 128), F32)], axis=0
+        ).astype(BF)
+        for j in range(4):
+            tables[g, j] = laid[j * 2 * SLOT : (j + 1) * 2 * SLOT]
 
     p1 = jnp.where(core == 0, x, y)
     p2 = jnp.where(core == 0, y, x)
@@ -355,13 +359,17 @@
 
     def step1(g):
         core_copy(g).wait_recv()
-        for j in range(4):
-            rows = slice((j % 2) * PART, (j % 2 + 1) * PART)
-            added = grads[g, 2 * core + j // 2, rows].astype(F32) + core_in[g, j // 2, rows].astype(F32)
+        def fill(j):
+            half = j // 2
+            rows = pl.ds(pl.multiple_of((j - 2 * half) * PART, PART), PART)
+            added = grads[g, 2 * core + half, rows].astype(F32) + core_in[g, half, rows].astype(F32)
             s1_out[g, j, :PART] = added.astype(BF)
-            s1_out[g, j, PART:] = tables[g, j].reshape(4 * SLOT, 128)
+            s1_out[g, j, PART:] = tables[g, j]
+
         for i in (2, 1, 3):
+            fill(after1(i))
             s1_copy(g, after1(i)).start()
+        fill(p1)
 
     def step2(g):
         def split(part, source):
@@ -377,7 +385,7 @@
             w, t0, t1 = w + more[0], t0 + more[1], t1 + more[2]
         for j in range(4):
             s2_out[g, j] = jnp.concatenate(
-                [w[j * PIECE : (j + 1) * PIECE], t0[j * SLOT : (j + 1) * SLOT], t1[j * SLOT : (j + 1) * SLOT]], axis=0
+                [w[j * PIECE : (j + 1) * PIECE], t0[j * UNIT : (j + 1) * UNIT], t1[j * UNIT : (j + 1) * UNIT]], axis=0
             ).astype(BF)
         for i in (2, 1, 3):
             s2_copy(g, after2(i)).start()
@@ -595,18 +603,24 @@
                                 part[u : u + SLOT]
                             )
 
+    count = GROUP * ROWS // UNIT
+    rest = WLAT * SPREAD - 128
     for b in range(4):
-        at = PIECE + (b // 2) * SLOT
-        for t in range(4):
-            stacked = jnp.concatenate(
-                [
-                    full[g, b % 2, slot // 4, slot % 4, at : at + SLOT]
-                    for g in range(groups)
-                    for slot in range(3 * t, 3 * t + 3)
-                ],
-                axis=0,
-            )
-            wide[b, :, t * 128 : (t + 1) * 128] = nn(reorder[...], stacked)
+        at = (b // 2) * UNIT
+        units = [
+            [full[g, b % 2, u // 4, u % 4, PIECE:].astype(F32)[at : at + UNIT] for u in range(2 * count + 1)]
+            for g in range(groups)
+        ]
+        for t in range(2):
+            tile = jnp.concatenate([u for g in range(groups) for u in units[g][t * count : (t + 1) * count]], axis=0)
+            wide[b, :, t * 256 : t * 256 + 128] = nn(reorder[...], tile.astype(BF))
+        ends = jnp.concatenate(
+            [units[g][2 * count][:, i * 2 * rest : (i + 1) * 2 * rest] for g in range(groups) for i in range(count)],
+            axis=0,
+        )
+        ends = nn(reorder[...], ends.astype(BF))
+        wide[b, :, 128 : 128 + rest] = ends[:, :rest]
+        wide[b, :, 384 : 384 + rest] = ends[:, rest:]
     for kind in range(4):
         band = jnp.int32(0)
         for b in range(1, 4):
@@ -644,7 +658,7 @@
     bf = lambda *shape: pltpu.VMEM(shape, BF)
     f32 = lambda *shape: pltpu.VMEM(shape, F32)
     pairs = lambda *shape: [dma(shape), dma(shape)]
-    pieces = (groups, 2, 4, 4, PIECE + 2 * SLOT, 128)
+    pieces = (groups, 2, 4, 4, PIECE + SLOT, 128)
     table = bias_table.transpose(1, 0, 2)
     joined, full, small = pl.pallas_call(
         whole_kernel,
@@ -682,13 +696,13 @@
             bf(WPL, half_lat, lon_cols, channels),
             bf(2, WPL, half_lat, EDGE, channels),
             bf(groups, 4, channels, 128),
-            bf(groups, 4, 4, SLOT, 128),
+            bf(groups, 4, 2 * SLOT, 128),
             bf(groups, 2, channels, 128),
-            bf(groups, 4, PART + 4 * SLOT, 128),
-            bf(groups, 4, PART + 4 * SLOT, 128),
-            bf(groups, 4, PIECE + 2 * SLOT, 128),
-            bf(groups, 4, PIECE + 2 * SLOT, 128),
-            bf(groups, Z_SIZE, PIECE + 2 * SLOT, 128),
+            bf(groups, 4, PART + 2 * SLOT, 128),
+            bf(groups, 4, PART + 2 * SLOT, 128),
+            bf(groups, 4, PIECE + SLOT, 128),
+            bf(groups, 4, PIECE + SLOT, 128),
+            bf(groups, Z_SIZE, PIECE + SLOT, 128),
             bf(*pieces),
             f32(8, 128),
             f32(8, 128),
@@ -724,7 +738,7 @@
             f32(*table.shape),
             dma((groups + 1,)),
         ],
-        compiler_params=pltpu.CompilerParams(vmem_limit_bytes=40 * 1024 * 1024),
+        compiler_params=pltpu.CompilerParams(vmem_limit_bytes=60 * 1024 * 1024),
         cost_estimate=pl.CostEstimate(flops=100_000_000, bytes_accessed=6_000_000, transcendentals=0),
     )(band_type, full, joined, small, constants[-1])
     return d_tokens, g_qkv, g_proj, g_gain, g_shift, g_table.transpose(1, 0, 2)

time: 72.9 us -> 81.2 us (1.11)
  Pallas kernels: 68.6 us -> 80.2 us
  local copies, waits for them, and re-layouts: 3.23 us -> 0 us
    pallas_call x1, Pallas kernels: 3.49 us -> 16.6 us  [local(): pl.pallas_call(assemble_kernel, out_shape=(jax.ShapeDtypeStruct(tokens.sh...]
    unnamed x10 -> x0, local copies, waits for them, and re-layouts: 3.23 us -> none
    pallas_call x1, Pallas kernels: 65.1 us -> 63.7 us  [local(): pl.pallas_call(whole_kernel, out_shape=(jax.ShapeDtypeStruct(tokens.shape...]
where the time goes in v1:
time: 81.2 us; the launch traced here: 81 us
  Pallas kernels  80.2 us (99%)
    pallas_call x1, Pallas kernels, local(): pl.pallas_call(whole_kernel, out_shape=(jax.ShapeDtypeStruct(tokens.shape...  63.7 us
    pallas_call x1, Pallas kernels, local(): pl.pallas_call(assemble_kernel, out_shape=(jax.ShapeDtypeStruct(tokens.sh...  16.6 us

profile of v1, /device:TPU:1, one launch (start us, length us, event | category | flops | bytes accessed | tf_op | source)
XLA Modules:
  0.0 81.0 jit_solution(5739262259348297486)
XLA Ops:
  0.6 63.7 %shard_map.199 = (bf16[2,6,48,384]{3,2,1,0:T(8,128)(2,1)}, bf16[3,2,4,4,64,128]{5,4,3,2,1,0:T(8,128)(2,1)}, f32[8,128]{1,0:T(8,128)}) custom-call(s32[2,6]{1,0:T(2,128)} %ids.1, s32[4]{0:T(128)} %types.3, bf16[2,6,48,384]{3,2,1,0:T(8,128)(2,1)} %tokens.1, bf16[2,6,48,384]{3,2,1,0:T(8,128)(2,1)} %cotangent.1, bf16[12,4,3312]{2,1,0:T(4,128)(2,1)} %bitcast.2, ...), custom_call_target="tpu_custom_call" | custom-call | flops 6000000000 | bytes 10000000 | tf_op jit(solution)/shard_map/pallas_call | solution.py:663
  64.3 16.6 %shard_map.200 = (bf16[2,6,48,384]{3,2,1,0:T(8,128)(2,1)}, bf16[384,1152]{1,0:T(8,128)(2,1)}, bf16[384,384]{1,0:T(8,128)(2,1)}, bf16[12,4,3312]{2,1,0:T(4,128)(2,1)}, f32[384]{0:T(512)}, /*index=5*/f32[384]{0:T(512)}) custom-call(s32[4]{0:T(128)} %types.3, bf16[3,2,4,4,64,128]{5,4,3,2,1,0:T(8,128)(2,1)} %get-tuple-element.15.full_h, ...), custom_call_target="tpu_custom_call" | custom-call | flops 100000000 | bytes 6000000 | tf_op jit(solution)/shard_map/pallas_call | solution.py:723

commit v2 on v1

--- a/solution.py
+++ b/solution.py
@@ -290,6 +290,8 @@
         proj = tn(att[:, g * 128 : (g + 1) * 128], cot[...]).astype(BF)
         for t in range(groups):
             grads[g, 3, t * 128 : (t + 1) * 128] = proj[:, t * 128 : (t + 1) * 128]
+
+    def fold(g):
         high = d_bias[...].astype(BF)
         low = (d_bias[...] - high.astype(F32)).astype(BF)
         spread = nt(high, perm[...]) + nt(low, perm[...])
@@ -486,6 +488,7 @@
         d_bias[...] += two_windows(g, 2)
         gradients(g)
         step0(g)
+        fold(g)
 
     def mid1():
         step1(0)
@@ -498,8 +501,8 @@
     group(1, mid1)
     group(2, mid2)
     step3(0)
+    step1(2)
     step2(1)
-    step1(2)
 
     d_ln = nt(d_qkv[...], w_qkv[...])
     norm = normed[...]
@@ -572,18 +575,21 @@
 def assemble_kernel(
     types, full_h, joined_h, small, reorder,
     o_tokens, o_qkv, o_proj, o_table, o_gain, o_shift,
-    full, wide, typed, sem,
+    full, joined, wide, typed, sem,
 ):
     channels = o_proj.shape[0]
     groups = channels // 128
     heads = groups * GROUP
     loads = [pltpu.make_async_copy(full_h.at[g], full.at[g], sem.at[g]) for g in range(groups)]
-    through = pltpu.make_async_copy(joined_h, o_tokens, sem.at[groups])
+    inward = pltpu.make_async_copy(joined_h, joined, sem.at[groups])
+    outward = pltpu.make_async_copy(joined, o_tokens, sem.at[groups + 1])
     for load in loads:
         load.start()
-    through.start()
+    inward.start()
     o_gain[...] = jnp.concatenate([small[g : g + 1] for g in range(groups)], axis=1).reshape(channels)
     o_shift[...] = jnp.concatenate([small[g : g + 1] for g in range(groups, 2 * groups)], axis=1).reshape(channels)
+    inward.wait()
+    outward.start()
     for g in range(groups):
         loads[g].wait()
         for half in range(2):
@@ -634,7 +640,7 @@
                     parts.append(table_rows[row : row + heads, lk * 256 : lk * 256 + WLAT * SPREAD])
         typed[:, kind, :] = jnp.concatenate(parts, axis=1)
     o_table[...] = typed[...].astype(BF)
-    through.wait()
+    outward.wait()
 
 
 def local(tokens, cotangent, mask_ids, band_type, bias_table, w_qkv, w_proj, ln_gain, ln_shift):
@@ -734,9 +740,10 @@
         out_specs=(anywhere, vmem, vmem, vmem, vmem, vmem),
         scratch_shapes=[
             bf(*pieces),
+            bf(*tokens.shape),
             f32(4, heads * ROWS, 512),
             f32(*table.shape),
-            dma((groups + 1,)),
+            dma((groups + 2,)),
         ],
         compiler_params=pltpu.CompilerParams(vmem_limit_bytes=60 * 1024 * 1024),
         cost_estimate=pl.CostEstimate(flops=100_000_000, bytes_accessed=6_000_000, transcendentals=0),

time: 81.2 us -> 67.7 us (0.83)
  Pallas kernels: 80.2 us -> 66.7 us
    pallas_call x1, Pallas kernels: 16.6 us -> 4.73 us  [local(): pl.pallas_call(assemble_kernel, out_shape=(jax.ShapeDtypeStruct(tokens.sh...]
    pallas_call x1, Pallas kernels: 63.7 us -> 62 us  [local(): pl.pallas_call(whole_kernel, out_shape=(jax.ShapeDtypeStruct(tokens.shape...]
where the time goes in v2:
time: 67.7 us; the launch traced here: 67.5 us
  Pallas kernels  66.7 us (99%)
  between operations  0.8 us (1%)
    pallas_call x1, Pallas kernels, local(): pl.pallas_call(whole_kernel, out_shape=(jax.ShapeDtypeStruct(tokens.shape...  62 us
    pallas_call x1, Pallas kernels, local(): pl.pallas_call(assemble_kernel, out_shape=(jax.ShapeDtypeStruct(tokens.sh...  4.73 us

profile of v2, /device:TPU:1, one launch (start us, length us, event | category | flops | bytes accessed | tf_op | source)
XLA Modules:
  0.0 67.5 jit_solution(10323315299957020567)
XLA Ops:
  0.6 62.0 %shard_map.199 = (bf16[2,6,48,384]{3,2,1,0:T(8,128)(2,1)}, bf16[3,2,4,4,64,128]{5,4,3,2,1,0:T(8,128)(2,1)}, f32[8,128]{1,0:T(8,128)}) custom-call(s32[2,6]{1,0:T(2,128)} %ids.1, s32[4]{0:T(128)} %types.3, bf16[2,6,48,384]{3,2,1,0:T(8,128)(2,1)} %tokens.1, bf16[2,6,48,384]{3,2,1,0:T(8,128)(2,1)} %cotangent.1, bf16[12,4,3312]{2,1,0:T(4,128)(2,1)} %bitcast.2, ...), custom_call_target="tpu_custom_call" | custom-call | flops 6000000000 | bytes 10000000 | tf_op jit(solution)/shard_map/pallas_call | solution.py:669
  62.6 4.7 %shard_map.200 = (bf16[2,6,48,384]{3,2,1,0:T(8,128)(2,1)}, bf16[384,1152]{1,0:T(8,128)(2,1)}, bf16[384,384]{1,0:T(8,128)(2,1)}, bf16[12,4,3312]{2,1,0:T(4,128)(2,1)}, f32[384]{0:T(512)}, /*index=5*/f32[384]{0:T(512)}) custom-call(s32[4]{0:T(128)} %types.3, bf16[3,2,4,4,64,128]{5,4,3,2,1,0:T(8,128)(2,1)} %get-tuple-element.15.full_h, ...), custom_call_target="tpu_custom_call" | custom-call | flops 100000000 | bytes 6000000 | tf_op jit(solution)/shard_map/pallas_call | solution.py:729

commit v3 on v2

--- a/solution.py
+++ b/solution.py
@@ -112,7 +112,7 @@
     route_h, unroute_h, perm_h, order_h, blocks_h, gather_h, reorder_h,
     o_tokens, o_full, o_small,
     cat, edge, cot_own, joined, table, w_qkv, w_proj, route, unroute, perm, order, blocks, gather, reorder,
-    tall, folded, bias, d_bias, normed, inv, ln, ln_t, cot, qkv, d_att, att, d_qkv,
+    tall, folded, summed, bias, d_bias, normed, inv, ln, ln_t, cot, qkv, d_att, att, d_qkv,
     d_main, d_edge, back_main, back_edge,
     grads, tables, core_in, s1_out, s1_in, s2_out, s2_in, z_in, full, small, small_core, small_x, small_y, small_z,
     load_s, out_s, halo_s, halo_r, back_s, back_r, core_s, core_r, s1_s, s1_r, s2_s, s2_r, z_s, z_r, g2_s, g2_r, g1_s, g1_r,
@@ -259,18 +259,17 @@
         raised = jnp.exp2(nt(k, q_heads) * (scale * LOG2E) + bias[g])
         probs = raised * (1.0 / jnp.sum(raised, axis=0, keepdims=True))
         probs_b = probs.astype(BF)
-        v_t = nt(eye, v).astype(BF)
-        k_t = nt(eye, k).astype(BF)
         weighted = probs * nt(v, da_heads)
         d_scores = weighted - probs * jnp.sum(weighted, axis=0, keepdims=True)
         d_scores_b = d_scores.astype(BF)
         mask = blocks[...]
-        att_t = nn(v_t, probs_b).astype(BF) * mask
-        dq_t = (nn(k_t, d_scores_b) * scale).astype(BF) * mask
+        att_t = tn(v, probs_b).astype(BF) * mask
+        dq_t = (tn(k, d_scores_b) * scale).astype(BF) * mask
 
         def store():
-            att[rows, cols] = nt(gather[...], att_t).astype(BF)
-            d_qkv[rows, q_cols] = nt(gather[...], dq_t).astype(BF)
+            joint = nt(gather[...], jnp.concatenate([att_t, dq_t], axis=0)).astype(BF)
+            att[rows, cols] = joint[:, :128]
+            d_qkv[rows, q_cols] = joint[:, 128:]
             d_qkv[rows, k_cols] = (nn(d_scores_b, q_heads) * scale).astype(BF)
             d_qkv[rows, v_cols] = nn(probs_b, da_heads).astype(BF)
 
@@ -292,14 +291,14 @@
             grads[g, 3, t * 128 : (t + 1) * 128] = proj[:, t * 128 : (t + 1) * 128]
 
     def fold(g):
-        high = d_bias[...].astype(BF)
-        low = (d_bias[...] - high.astype(F32)).astype(BF)
-        spread = nt(high, perm[...]) + nt(low, perm[...])
-        folded[:, :128] = jnp.zeros((folded.shape[0], 128), F32)
+        spread = nt(d_bias[...].astype(BF), perm[...])
+        for part in range(2):
+            summed[part] = jnp.zeros(summed.shape[1:], F32)
         for o in range(WLON):
             start = (WLON - 1 - o) * ROWS
-            folded[start : start + WINDOW, : GROUP * ROWS] += spread[:, o * GROUP * ROWS : (o + 1) * GROUP * ROWS]
-        rows = tn(folded[:, : GROUP * ROWS].astype(BF), order[...])
+            summed[o % 2, start : start + WINDOW, : GROUP * ROWS] += spread[:, o * GROUP * ROWS : (o + 1) * GROUP * ROWS]
+        laid = summed[0, :, : GROUP * ROWS] + summed[1, :, : GROUP * ROWS]
+        rows = tn(laid.astype(BF), order[...])
         rest = WLAT * SPREAD - 128
         ends = jnp.concatenate([rows[:, 128 : 128 + rest], rows[:, 384 : 384 + rest]], axis=1)
         count = GROUP * ROWS // UNIT
@@ -574,8 +573,8 @@
 
 def assemble_kernel(
     types, full_h, joined_h, small, reorder,
-    o_tokens, o_qkv, o_proj, o_table, o_gain, o_shift,
-    full, joined, wide, typed, sem,
+    o_tokens, qkv_h, proj_h, o_table, o_gain, o_shift,
+    full, joined, o_qkv, o_proj, wide, typed, sem,
 ):
     channels = o_proj.shape[0]
     groups = channels // 128
@@ -609,6 +608,12 @@
                                 part[u : u + SLOT]
                             )
 
+    results = [
+        pltpu.make_async_copy(o_qkv, qkv_h, sem.at[groups + 2]), pltpu.make_async_copy(o_proj, proj_h, sem.at[groups + 3])
+    ]
+    for result in results:
+        result.start()
+
     count = GROUP * ROWS // UNIT
     rest = WLAT * SPREAD - 128
     for b in range(4):
@@ -641,6 +646,8 @@
         typed[:, kind, :] = jnp.concatenate(parts, axis=1)
     o_table[...] = typed[...].astype(BF)
     outward.wait()
+    for result in results:
+        result.wait()
 
 
 def local(tokens, cotangent, mask_ids, band_type, bias_table, w_qkv, w_proj, ln_gain, ln_shift):
@@ -686,6 +693,7 @@
             *[bf(*c.shape) for c in constants],
             f32(heads * ROWS, 512),
             f32(SPREAD * ROWS, heads * ROWS),
+            f32(2, SPREAD * ROWS, 128),
             f32(groups, WINDOW, span),
             f32(WINDOW, span),
             f32(count, channels),
@@ -737,13 +745,15 @@
             jax.ShapeDtypeStruct((channels,), F32),
         ),
         in_specs=[scalars, anywhere, anywhere, vmem, vmem],
-        out_specs=(anywhere, vmem, vmem, vmem, vmem, vmem),
+        out_specs=(anywhere, anywhere, anywhere, vmem, vmem, vmem),
         scratch_shapes=[
             bf(*pieces),
             bf(*tokens.shape),
+            bf(channels, 3 * channels),
+            bf(channels, channels),
             f32(4, heads * ROWS, 512),
             f32(*table.shape),
-            dma((groups + 2,)),
+            dma((groups + 4,)),
         ],
         compiler_params=pltpu.CompilerParams(vmem_limit_bytes=60 * 1024 * 1024),
         cost_estimate=pl.CostEstimate(flops=100_000_000, bytes_accessed=6_000_000, transcendentals=0),

time: 67.7 us -> 67.9 us (level)
  no operation moved by 1% of the time
where the time goes in v3:
time: 67.9 us; the launch traced here: 67.8 us
  Pallas kernels  66.9 us (99%)
  between operations  0.8 us (1%)
    pallas_call x1, Pallas kernels, local(): pl.pallas_call(whole_kernel, out_shape=(jax.ShapeDtypeStruct(tokens.shape...  61.7 us
    pallas_call x1, Pallas kernels, local(): pl.pallas_call(assemble_kernel, out_shape=(jax.ShapeDtypeStruct(tokens.sh...  5.28 us

profile of v3, /device:TPU:1, one launch (start us, length us, event | category | flops | bytes accessed | tf_op | source)
XLA Modules:
  0.0 67.8 jit_solution(3506439741914841713)
XLA Ops:
  0.6 61.7 %shard_map.199 = (bf16[2,6,48,384]{3,2,1,0:T(8,128)(2,1)}, bf16[3,2,4,4,64,128]{5,4,3,2,1,0:T(8,128)(2,1)}, f32[8,128]{1,0:T(8,128)}) custom-call(s32[2,6]{1,0:T(2,128)} %ids.1, s32[4]{0:T(128)} %types.3, bf16[2,6,48,384]{3,2,1,0:T(8,128)(2,1)} %tokens.1, bf16[2,6,48,384]{3,2,1,0:T(8,128)(2,1)} %cotangent.1, bf16[12,4,3312]{2,1,0:T(4,128)(2,1)} %bitcast.2, ...), custom_call_target="tpu_custom_call" | custom-call | flops 6000000000 | bytes 10000000 | tf_op jit(solution)/shard_map/pallas_call | solution.py:676
  62.3 5.3 %shard_map.200 = (bf16[2,6,48,384]{3,2,1,0:T(8,128)(2,1)}, bf16[384,1152]{1,0:T(8,128)(2,1)}, bf16[384,384]{1,0:T(8,128)(2,1)}, bf16[12,4,3312]{2,1,0:T(4,128)(2,1)}, f32[384]{0:T(512)}, /*index=5*/f32[384]{0:T(512)}) custom-call(s32[4]{0:T(128)} %types.3, bf16[3,2,4,4,64,128]{5,4,3,2,1,0:T(8,128)(2,1)} %get-tuple-element.15.full_h, ...), custom_call_target="tpu_custom_call" | custom-call | flops 100000000 | bytes 6000000 | tf_op jit(solution)/shard_map/pallas_call | solution.py:737

commit v4 on v3

--- a/solution.py
+++ b/solution.py
@@ -489,18 +489,16 @@
         step0(g)
         fold(g)
 
-    def mid1():
-        step1(0)
-
-    def mid2():
-        step1(1)
-        step2(0)
-
-    group(0, lambda: None)
-    group(1, mid1)
-    group(2, mid2)
+    def nothing():
+        pass
+
+    group(0, nothing)
+    step1(0)
+    group(1, nothing)
+    step1(1)
+    group(2, lambda: step2(0))
+    step1(2)
     step3(0)
-    step1(2)
     step2(1)
 
     d_ln = nt(d_qkv[...], w_qkv[...])
@@ -573,8 +571,8 @@
 
 def assemble_kernel(
     types, full_h, joined_h, small, reorder,
-    o_tokens, qkv_h, proj_h, o_table, o_gain, o_shift,
-    full, joined, o_qkv, o_proj, wide, typed, sem,
+    o_tokens, o_qkv, o_proj, o_table, o_gain, o_shift,
+    full, joined, wide, typed, sem,
 ):
     channels = o_proj.shape[0]
     groups = channels // 128
@@ -608,12 +606,6 @@
                                 part[u : u + SLOT]
                             )
 
-    results = [
-        pltpu.make_async_copy(o_qkv, qkv_h, sem.at[groups + 2]), pltpu.make_async_copy(o_proj, proj_h, sem.at[groups + 3])
-    ]
-    for result in results:
-        result.start()
-
     count = GROUP * ROWS // UNIT
     rest = WLAT * SPREAD - 128
     for b in range(4):
@@ -646,8 +638,6 @@
         typed[:, kind, :] = jnp.concatenate(parts, axis=1)
     o_table[...] = typed[...].astype(BF)
     outward.wait()
-    for result in results:
-        result.wait()
 
 
 def local(tokens, cotangent, mask_ids, band_type, bias_table, w_qkv, w_proj, ln_gain, ln_shift):
@@ -745,15 +735,13 @@
             jax.ShapeDtypeStruct((channels,), F32),
         ),
         in_specs=[scalars, anywhere, anywhere, vmem, vmem],
-        out_specs=(anywhere, anywhere, anywhere, vmem, vmem, vmem),
+        out_specs=(anywhere, vmem, vmem, vmem, vmem, vmem),
         scratch_shapes=[
             bf(*pieces),
             bf(*tokens.shape),
-            bf(channels, 3 * channels),
-            bf(channels, channels),
             f32(4, heads * ROWS, 512),
             f32(*table.shape),
-            dma((groups + 4,)),
+            dma((groups + 2,)),
         ],
         compiler_params=pltpu.CompilerParams(vmem_limit_bytes=60 * 1024 * 1024),
         cost_estimate=pl.CostEstimate(flops=100_000_000, bytes_accessed=6_000_000, transcendentals=0),

time: 67.9 us -> 67.1 us (0.988)
  Pallas kernels: 66.9 us -> 66.1 us
where the time goes in v4:
time: 67.1 us; the launch traced here: 66.9 us
  Pallas kernels  66.1 us (99%)
  between operations  0.8 us (1%)
    pallas_call x1, Pallas kernels, local(): pl.pallas_call(whole_kernel, out_shape=(jax.ShapeDtypeStruct(tokens.shape...  61.4 us
    pallas_call x1, Pallas kernels, local(): pl.pallas_call(assemble_kernel, out_shape=(jax.ShapeDtypeStruct(tokens.sh...  4.73 us

profile of v4, /device:TPU:1, one launch (start us, length us, event | category | flops | bytes accessed | tf_op | source)
XLA Modules:
  0.0 66.9 jit_solution(5053682690372283301)
XLA Ops:
  0.6 61.4 %shard_map.199 = (bf16[2,6,48,384]{3,2,1,0:T(8,128)(2,1)}, bf16[3,2,4,4,64,128]{5,4,3,2,1,0:T(8,128)(2,1)}, f32[8,128]{1,0:T(8,128)}) custom-call(s32[2,6]{1,0:T(2,128)} %ids.1, s32[4]{0:T(128)} %types.3, bf16[2,6,48,384]{3,2,1,0:T(8,128)(2,1)} %tokens.1, bf16[2,6,48,384]{3,2,1,0:T(8,128)(2,1)} %cotangent.1, bf16[12,4,3312]{2,1,0:T(4,128)(2,1)} %bitcast.2, ...), custom_call_target="tpu_custom_call" | custom-call | flops 6000000000 | bytes 10000000 | tf_op jit(solution)/shard_map/pallas_call | solution.py:666
  62.0 4.7 %shard_map.200 = (bf16[2,6,48,384]{3,2,1,0:T(8,128)(2,1)}, bf16[384,1152]{1,0:T(8,128)(2,1)}, bf16[384,384]{1,0:T(8,128)(2,1)}, bf16[12,4,3312]{2,1,0:T(4,128)(2,1)}, f32[384]{0:T(512)}, /*index=5*/f32[384]{0:T(512)}) custom-call(s32[4]{0:T(128)} %types.3, bf16[3,2,4,4,64,128]{5,4,3,2,1,0:T(8,128)(2,1)} %get-tuple-element.15.full_h, ...), custom_call_target="tpu_custom_call" | custom-call | flops 100000000 | bytes 6000000 | tf_op jit(solution)/shard_map/pallas_call | solution.py:727

commit v5 on v4

--- a/solution.py
+++ b/solution.py
@@ -425,17 +425,18 @@
             source = after1(i)
             g1_copy(g, source, source).wait_recv()
             sib_copy(g, core, source).start()
+        full_copy(g, core, 0).start()
 
     def step7(g):
         for i in range(4):
             sib_copy(g, other, i).wait_recv()
-        full_copy(g).start()
-
-    def full_copy(g):
-        return pltpu.make_async_copy(full.at[g], o_full.at[g], out_s.at[g])
+        full_copy(g, other, 1).start()
+
+    def full_copy(g, half, i):
+        return pltpu.make_async_copy(full.at[g, half], o_full.at[g, half], out_s.at[2 * g + i])
 
     def tokens_copy():
-        return pltpu.make_async_copy(joined, o_tokens, out_s.at[groups])
+        return pltpu.make_async_copy(joined, o_tokens, out_s.at[2 * groups])
 
     def finish(g):
         core_copy(g).wait_send()
@@ -443,9 +444,12 @@
             s1_copy(g, after1(i)).wait_send()
             s2_copy(g, after2(i)).wait_send()
             g2_copy(g, after2(i), p2).wait_send()
-            g1_copy(g, after1(i), p1).wait_send()
         for i in range(1, Z_SIZE):
             z_copy(g, lax.rem(z + i, Z_SIZE), z).wait_send()
+
+    def finish_gather(g):
+        for i in range(1, 4):
+            g1_copy(g, after1(i), p1).wait_send()
         for i in range(4):
             sib_copy(g, core, i).wait_send()
 
@@ -556,17 +560,21 @@
     step5(2)
     step6(1)
     step7(1)
+
+    for copy in halos + backs:
+        copy.wait_send()
+    small_finish()
+    for g in range(groups):
+        finish(g)
+    finish_gather(0)
+    finish_gather(1)
     step6(2)
     step7(2)
-
-    for copy in halos + backs:
-        copy.wait_send()
-    for g in range(groups):
-        finish(g)
-    small_finish()
+    finish_gather(2)
     tokens_copy().wait()
     for g in range(groups):
-        full_copy(g).wait()
+        full_copy(g, core, 0).wait()
+        full_copy(g, other, 1).wait()
 
 
 def assemble_kernel(
@@ -714,7 +722,7 @@
             f32(Y_SIZE, 8, 128),
             f32(Z_SIZE, 8, 128),
             dma((12 + 3 * groups,)),
-            dma((groups + 1,)),
+            dma((2 * groups + 1,)),
             *pairs(6), *pairs(3), *pairs(groups), *pairs(groups, 4), *pairs(groups, 4), *pairs(groups, Z_SIZE),
             *pairs(groups, 4), *pairs(groups, 4), *pairs(groups, 4),
             *pairs(1), *pairs(X_SIZE), *pairs(Y_SIZE), *pairs(Z_SIZE),

time: 67.1 us -> 67 us (level)
  no operation moved by 1% of the time
where the time goes in v5:
time: 67 us; the launch traced here: 66.8 us
  Pallas kernels  66 us (99%)
  between operations  0.8 us (1%)
    pallas_call x1, Pallas kernels, local(): pl.pallas_call(whole_kernel, out_shape=(jax.ShapeDtypeStruct(tokens.shape...  61.3 us
    pallas_call x1, Pallas kernels, local(): pl.pallas_call(assemble_kernel, out_shape=(jax.ShapeDtypeStruct(tokens.sh...  4.73 us

profile of v5, /device:TPU:1, one launch (start us, length us, event | category | flops | bytes accessed | tf_op | source)
XLA Modules:
  0.0 66.8 jit_solution(7706805750020089890)
XLA Ops:
  0.6 61.3 %shard_map.199 = (bf16[2,6,48,384]{3,2,1,0:T(8,128)(2,1)}, bf16[3,2,4,4,64,128]{5,4,3,2,1,0:T(8,128)(2,1)}, f32[8,128]{1,0:T(8,128)}) custom-call(s32[2,6]{1,0:T(2,128)} %ids.1, s32[4]{0:T(128)} %types.3, bf16[2,6,48,384]{3,2,1,0:T(8,128)(2,1)} %tokens.1, bf16[2,6,48,384]{3,2,1,0:T(8,128)(2,1)} %cotangent.1, bf16[12,4,3312]{2,1,0:T(4,128)(2,1)} %bitcast.2, ...), custom_call_target="tpu_custom_call" | custom-call | flops 6000000000 | bytes 10000000 | tf_op jit(solution)/shard_map/pallas_call | solution.py:674
  61.9 4.7 %shard_map.200 = (bf16[2,6,48,384]{3,2,1,0:T(8,128)(2,1)}, bf16[384,1152]{1,0:T(8,128)(2,1)}, bf16[384,384]{1,0:T(8,128)(2,1)}, bf16[12,4,3312]{2,1,0:T(4,128)(2,1)}, f32[384]{0:T(512)}, /*index=5*/f32[384]{0:T(512)}) custom-call(s32[4]{0:T(128)} %types.3, bf16[3,2,4,4,64,128]{5,4,3,2,1,0:T(8,128)(2,1)} %get-tuple-element.15.full_h, ...), custom_call_target="tpu_custom_call" | custom-call | flops 100000000 | bytes 6000000 | tf_op jit(solution)/shard_map/pallas_call | solution.py:735

commit v6 on v5

--- a/solution.py
+++ b/solution.py
@@ -296,8 +296,11 @@
             summed[part] = jnp.zeros(summed.shape[1:], F32)
         for o in range(WLON):
             start = (WLON - 1 - o) * ROWS
+            start += start % UNIT
             summed[o % 2, start : start + WINDOW, : GROUP * ROWS] += spread[:, o * GROUP * ROWS : (o + 1) * GROUP * ROWS]
-        laid = summed[0, :, : GROUP * ROWS] + summed[1, :, : GROUP * ROWS]
+        shifted = UNIT // 2
+        rows = SPREAD * ROWS
+        laid = summed[0, shifted : shifted + rows, : GROUP * ROWS] + summed[1, :rows, : GROUP * ROWS]
         rows = tn(laid.astype(BF), order[...])
         rest = WLAT * SPREAD - 128
         ends = jnp.concatenate([rows[:, 128 : 128 + rest], rows[:, 384 : 384 + rest]], axis=1)
@@ -529,8 +532,8 @@
     ]
     for copy in backs:
         copy.start()
+    step2(2)
     step3(1)
-    step2(2)
     mc_copy().wait_recv()
     small_share(mx_copy, small_x, x, X_SIZE, small[...] + small_core[...])
     step4(0)
@@ -552,8 +555,8 @@
             joined[l, a, :EDGE] = (value[:EDGE] + outer.astype(F32)).astype(BF)
     tokens_copy().start()
     step4(1)
+    step4(2)
     step6(0)
-    step4(2)
     step5(1)
     step7(0)
     o_small[...] = small_sum(mz_copy, small_z, z, Z_SIZE)
@@ -691,7 +694,7 @@
             *[bf(*c.shape) for c in constants],
             f32(heads * ROWS, 512),
             f32(SPREAD * ROWS, heads * ROWS),
-            f32(2, SPREAD * ROWS, 128),
+            f32(2, SPREAD * ROWS + UNIT // 2, 128),
             f32(groups, WINDOW, span),
             f32(WINDOW, span),
             f32(count, channels),

time: 67 us -> 67 us (level)
  no operation moved by 1% of the time
where the time goes in v6:
time: 67 us; the launch traced here: 66.8 us
  Pallas kernels  66 us (99%)
  between operations  0.8 us (1%)
    pallas_call x1, Pallas kernels, local(): pl.pallas_call(whole_kernel, out_shape=(jax.ShapeDtypeStruct(tokens.shape...  61.3 us
    pallas_call x1, Pallas kernels, local(): pl.pallas_call(assemble_kernel, out_shape=(jax.ShapeDtypeStruct(tokens.sh...  4.73 us

profile of v6, /device:TPU:1, one launch (start us, length us, event | category | flops | bytes accessed | tf_op | source)
XLA Modules:
  0.0 66.8 jit_solution(3369661241674017810)
XLA Ops:
  0.6 61.3 %shard_map.199 = (bf16[2,6,48,384]{3,2,1,0:T(8,128)(2,1)}, bf16[3,2,4,4,64,128]{5,4,3,2,1,0:T(8,128)(2,1)}, f32[8,128]{1,0:T(8,128)}) custom-call(s32[2,6]{1,0:T(2,128)} %ids.1, s32[4]{0:T(128)} %types.3, bf16[2,6,48,384]{3,2,1,0:T(8,128)(2,1)} %tokens.1, bf16[2,6,48,384]{3,2,1,0:T(8,128)(2,1)} %cotangent.1, bf16[12,4,3312]{2,1,0:T(4,128)(2,1)} %bitcast.2, ...), custom_call_target="tpu_custom_call" | custom-call | flops 6000000000 | bytes 10000000 | tf_op jit(solution)/shard_map/pallas_call | solution.py:677
  61.9 4.7 %shard_map.200 = (bf16[2,6,48,384]{3,2,1,0:T(8,128)(2,1)}, bf16[384,1152]{1,0:T(8,128)(2,1)}, bf16[384,384]{1,0:T(8,128)(2,1)}, bf16[12,4,3312]{2,1,0:T(4,128)(2,1)}, f32[384]{0:T(512)}, /*index=5*/f32[384]{0:T(512)}) custom-call(s32[4]{0:T(128)} %types.3, bf16[3,2,4,4,64,128]{5,4,3,2,1,0:T(8,128)(2,1)} %get-tuple-element.15.full_h, ...), custom_call_target="tpu_custom_call" | custom-call | flops 100000000 | bytes 6000000 | tf_op jit(solution)/shard_map/pallas_call | solution.py:738
